TPU v7x, 32 devices: a whole 2x2x4 slice. The times are simulated.
32 devices in a mesh: row: 8 (over y, x, core), col: 4 (over z).
Axes of the slice: x: 2, y: 2, z: 4, core: 2. Of those that a mesh axis runs over, the one named last changes fastest.
Arguments:
- embeddings: bfloat16 [4096, 256], P(('row', 'col')), may hold values from -6 to 6
- cotangent: bfloat16 [4096, 256], P(('row', 'col')), may hold values from -6 to 6
- weight: bfloat16 [256, 256], replicated, may hold values from -0.375 to 0.375
- tiles: bfloat16 [32, 128, 128, 128], P(('row', 'col')), may hold values from -0.078125 to 0.078125
- tile_dst: int32 [32, 128], P(('row', 'col')), may hold values from 0 to 3
- tile_src: int32 [32, 128], P(('row', 'col')), may hold values from 0 to 7
- tile_count: int32 [32], P(('row', 'col')), may hold values from 1 to 128, as said below
Outputs:
- output: bfloat16 [4096, 256], P(('row', 'col'))
- grad_embeddings: bfloat16 [4096, 256], P(('row', 'col'))
- grad_weight: float32 [256, 256], replicated
Inputs may be any that keep to these rules, and one draw needn't show every extreme that they name: `tile_count`: at least one device has exactly 128 live slots.
All inputs are finite; a program needn't handle non-finite values.
Results may differ from a plain program's by a relative error of at most 0.012.
Values may be sent and summed in bfloat16 or wider, within the bound.
A program may use at most 128 MiB of HBM per device.

v0:
```python
import math
import jax
import jax.numpy as jnp
from jax import lax
from jax.sharding import PartitionSpec as P


def shards(embeddings, cotangent, weight, tiles, tile_dst, tile_src, tile_count):
    highest = lax.Precision.HIGHEST
    block_rows = embeddings.shape[0]
    feature_width = embeddings.shape[1]
    row_count = lax.axis_size("row")
    column_count = lax.axis_size("col")
    local_tiles = tiles[0]
    dest_ids = tile_dst[0]
    source_ids = tile_src[0]
    slot_ids = jnp.arange(local_tiles.shape[0], dtype=jnp.int32)
    alive_slots = (slot_ids < tile_count[0]).astype(jnp.float32)
    dest_onehot = (dest_ids[:, None] == jnp.arange(column_count, dtype=jnp.int32)[None, :]).astype(
        jnp.float32
    ) * alive_slots[:, None]
    source_onehot = (source_ids[:, None] == jnp.arange(row_count, dtype=jnp.int32)[None, :]).astype(
        jnp.float32
    ) * alive_slots[:, None]
    gathered = lax.all_gather(embeddings, "row", axis=0, tiled=True).reshape(
        row_count, block_rows, feature_width
    )
    chosen = jnp.take(gathered, source_ids, axis=0)
    products = jnp.einsum("tij,tjd->tid", local_tiles, chosen, preferred_element_type=jnp.float32)
    partial_value = jnp.einsum("tc,tid->cid", dest_onehot, products, precision=highest)
    partial_rounded = partial_value.astype(jnp.bfloat16).reshape(
        column_count * block_rows, feature_width
    )
    summed = lax.psum_scatter(
        partial_rounded.astype(jnp.float32).astype(jnp.bfloat16),
        "col",
        scatter_dimension=0,
        tiled=True,
    ).astype(jnp.float32)
    hidden = summed.astype(jnp.bfloat16)
    output = jnp.dot(hidden, weight, preferred_element_type=jnp.float32).astype(jnp.bfloat16)
    user_count = block_rows * row_count * column_count
    scale_factor = 1.0 / math.sqrt(user_count)
    contract_rows = (((0,), (0,)), ((), ()))
    contract_cols = (((1,), (1,)), ((), ()))
    grad_hidden = lax.dot_general(
        cotangent, weight, contract_cols, preferred_element_type=jnp.float32
    ).astype(jnp.bfloat16)
    grad_group = lax.all_gather(grad_hidden, "col", axis=0, tiled=True)
    weight_term = lax.dot_general(
        summed, cotangent.astype(jnp.float32), contract_rows, precision=highest
    )
    grad_weight = lax.psum(weight_term, ("row", "col")) * scale_factor
    dest_rows = grad_group.reshape(column_count, block_rows, feature_width)
    picked = jnp.take(dest_rows, dest_ids, axis=0)
    back_products = jnp.einsum(
        "tji,tjd->tid", local_tiles, picked, preferred_element_type=jnp.float32
    )
    back_partial = jnp.einsum("tr,tid->rid", source_onehot, back_products, precision=highest)
    back_rounded = lax.optimization_barrier(back_partial.astype(jnp.bfloat16)).astype(jnp.float32)
    back_summed = lax.psum_scatter(
        back_rounded.reshape(row_count * block_rows, feature_width).astype(jnp.bfloat16),
        "row",
        scatter_dimension=0,
        tiled=True,
    )
    return (output, back_summed, grad_weight)


def solution(mesh):
    in_specs = (
        P(("row", "col"), None),
        P(("row", "col"), None),
        P(),
        P(("row", "col"), None, None, None),
        P(("row", "col"), None),
        P(("row", "col"), None),
        P(("row", "col")),
    )
    out_specs = (P(("row", "col"), None), P(("row", "col"), None), P())
    return jax.shard_map(shards, mesh=mesh, in_specs=in_specs, out_specs=out_specs, check_vma=False)
```

profile of v0, /device:TPU:0, one launch (start us, length us, event | category | flops | bytes accessed | tf_op | source)
XLA Modules:
  0.0 260.4 jit_solution(8117860961400061152)
XLA Ops:
  8.0 0.0 reduce-scatter.3.cloned.1.call-start
  8.1 0.7 fusion.30
  8.7 0.7 compare_and_fusion.1
  9.4 11.6 %all_gather.6 = bf16[1024,256]{1,0:T(8,128)(2,1)S(1)} all-gather(bf16[128,256]{1,0:T(8,128)(2,1)} %param.7), channel_id=1, replica_groups=mesh['row'=8,'col'=4] {'row'}, dimensions={0}, use_global_device_ids=true | all-gather | bytes 589824 | tf_op jit(solution)/shard_map/all_gather | solution.py:25
  21.0 6.5 %gather_fusion = bf16[128,128,256]{2,1,0:T(8,128)(2,1)} fusion(bf16[8,128,256]{2,1,0:T(8,128)(2,1)S(1)} %bitcast.46, s32[1024]{0:T(1024)S(1)} %pad_clamp_fusion.1), kind=kCustom, calls=%fused_computation | custom fusion | bytes 16777728 | tf_op jit(solution)/shard_map/jit(_take)/gather | solution.py:28
  27.5 13.1 %fusion.6 = f32[128,256,128]{2,1,0:T(8,128)} fusion(bf16[128,128,256]{2,1,0:T(8,128)(2,1)} %gather_fusion, pred[128]{0:T(512)(128)(4,1)S(1)} %compare_and_fusion.1, bf16[1,128,128,128]{3,2,1,0:T(8,128)(2,1)} %param.10), kind=kOutput, calls=%fused_computation.8 | convolution fusion | flops 1077936128 | bytes 29360256 | tf_op jit(solution)/shard_map/tij,tjd->tid/dot_general | solution.py:29
  40.6 17.7 %copy.12 = f32[128,256,128]{1,0,2:T(8,128)} copy(f32[128,256,128]{2,1,0:T(8,128)} %fusion.6) | data formatting | bytes 33554432 | tf_op jit(solution)/shard_map/tij,tjd->tid/dot_general | solution.py:29
  59.0 10.8 %fusion.17 = bf16[4,128,256]{2,0,1:T(4,128)(2,1)S(1)} fusion(f32[128,256,128]{1,0,2:T(8,128)} %copy.12, f32[128]{0:T(128)S(1)} %compare_convert_fusion, s32[128]{0:T(128)S(1)} %bitcast.49), kind=kOutput, calls=%fused_computation.17 | convolution fusion | flops 201458688 | bytes 17040384 | tf_op jit(solution)/shard_map/tc,tid->cid/dot_general | solution.py:30
  69.8 0.7 copy.10
  70.6 0.0 reduce-scatter.3.cloned.1.call-update
  70.6 0.0 all-reduce.2.cloned.1.call-start
  70.7 0.2 convolution_convert_fusion
  70.9 15.5 %all_gather.7 = bf16[512,256]{1,0:T(8,128)(2,1)S(1)} all-gather(bf16[128,256]{1,0:T(8,128)(2,1)S(1)} %convolution_convert_fusion), channel_id=1, replica_groups=mesh['row'=8,'col'=4] {'col'}, dimensions={0}, use_global_device_ids=true | all-gather | bytes 327680 | tf_op jit(solution)/shard_map/all_gather | solution.py:49
  86.4 6.5 %gather_fusion.1 = bf16[128,128,256]{2,1,0:T(8,128)(2,1)} fusion(bf16[4,128,256]{2,1,0:T(8,128)(2,1)S(1)} %bitcast.45, s32[1024]{0:T(1024)S(1)} %pad_clamp_fusion), kind=kCustom, calls=%fused_computation.1 | custom fusion | bytes 16777728 | tf_op jit(solution)/shard_map/jit(_take)/gather | solution.py:55
  92.9 12.8 %fusion.4 = f32[128,256,128]{2,1,0:T(8,128)} fusion(bf16[128,128,256]{2,1,0:T(8,128)(2,1)} %gather_fusion.1, pred[128]{0:T(512)(128)(4,1)S(1)} %compare_and_fusion, bf16[1,128,128,128]{3,2,1,0:T(8,128)(2,1)} %param.10), kind=kOutput, calls=%fused_computation.6 | convolution fusion | flops 1077936128 | bytes 29360256 | tf_op jit(solution)/shard_map/tji,tjd->tid/dot_general | solution.py:56
  105.7 17.7 %copy.13 = f32[128,256,128]{1,0,2:T(8,128)} copy(f32[128,256,128]{2,1,0:T(8,128)} %fusion.4) | data formatting | bytes 33554432 | tf_op jit(solution)/shard_map/tji,tjd->tid/dot_general | solution.py:56
  123.4 1.7 fusion.36
  125.2 0.0 reduce-scatter.5.cloned.1.call-start
  125.2 10.8 %fusion.14 = bf16[8,128,256]{2,0,1:T(8,128)(2,1)S(1)} fusion(f32[128,256,128]{1,0,2:T(8,128)} %copy.13, f32[128]{0:T(128)S(1)} %compare_convert_fusion, s32[128]{0:T(128)S(1)} %bitcast.50), kind=kOutput, calls=%fused_computation.16 | convolution fusion | flops 402917376 | bytes 17302528 | tf_op jit(solution)/shard_map/tr,tid->rid/dot_general | solution.py:59
  136.1 0.9 copy.11
  137.0 0.0 reduce-scatter.5.cloned.1.call-update
  137.0 0.8 convolution_convert_fusion.1
  137.8 113.4 %all-reduce.2.cloned.1.call-done = f32[256,256]{1,0:T(8,128)} async-done(((f32[256,256]{1,0:T(8,128)}), f32[256,256]{1,0:T(8,128)}) %all-reduce.2.cloned.1.call-update) | async-done | bytes 262160 | tf_op jit(solution)/shard_map/psum | solution.py:53
  251.3 1.7 broadcast_multiply_fusion
  (18 shorter events, 0.1 us)
Async XLA Ops:
  8.0 62.7 %copy-start = (bf16[256,256]{1,0:T(8,128)(2,1)S(1)}, bf16[256,256]{1,0:T(8,128)(2,1)}, u32[]{:S(2)}) copy-start(bf16[256,256]{1,0:T(8,128)(2,1)} %param.9) | copy-start | bytes 393220
  8.0 115.4 %reduce-scatter.3.cloned.1.call-start = ((), (), s32[]{:S(2)}) async-start(), calls=%async_computation.2 | async-start | bytes 327680 | tf_op jit(solution)/shard_map/reduce_scatter | solution.py:34
  40.6 18.4 %copy-start.3 = (s32[1,128]{1,0:T(1,128)S(1)}, s32[1,128]{1,0:T(1,128)}, u32[]{:S(2)}) copy-start(s32[1,128]{1,0:T(1,128)} %param.11) | copy-start | bytes 1540
  59.0 11.7 %copy-start.1 = (bf16[128,256]{1,0:T(8,128)(2,1)S(1)}, bf16[128,256]{1,0:T(8,128)(2,1)}, u32[]{:S(2)}) copy-start(bf16[128,256]{1,0:T(8,128)(2,1)} %param.8) | copy-start | bytes 196612
  70.6 180.7 %all-reduce.2.cloned.1.call-start = ((), (), s32[]{:S(2)}) async-start(), calls=%async_computation.4 | async-start | bytes 524288 | tf_op jit(solution)/shard_map/psum | solution.py:53
  105.7 19.5 %copy-start.4 = (s32[1,128]{1,0:T(1,128)S(1)}, s32[1,128]{1,0:T(1,128)}, u32[]{:S(2)}) copy-start(s32[1,128]{1,0:T(1,128)} %param.12) | copy-start | bytes 1540
  125.2 127.8 %reduce-scatter.5.cloned.1.call-start = ((), (), s32[]{:S(2)}) async-start(), calls=%async_computation.3 | async-start | bytes 589824 | tf_op jit(solution)/shard_map/reduce_scatter | solution.py:61
  125.2 11.8 %copy-start.2 = (bf16[128,256]{1,0:T(8,128)(2,1)S(1)}, bf16[128,256]{1,0:T(8,128)(2,1)}, u32[]{:S(2)}) copy-start(bf16[128,256]{1,0:T(8,128)(2,1)} %reduce-scatter.3.cloned.1.call-done) | copy-start | bytes 196612
Sparse Core Ops, SparseCore 0:
  70.7 20.6 reduce-scatter.2
  125.3 125.9 all-reduce.1
Sparse Core Ops, SparseCore 1:
  137.1 34.8 reduce-scatter.4
where the time goes:
time: 261 us; the launch traced here: 260 us
  waiting for transfers between devices  113 us (43%)
  matrix products  50.3 us (19%)
  local copies, waits for them, and re-layouts  50 us (19%)
  blocking collectives  27.1 us (10%)
  between operations  16.3 us (6%)
  other arithmetic  3.05 us (1%)
    psum x1, waiting for transfers between devices, shards(): grad_weight = lax.psum(weight_term, ('row', 'col')) * scale_factor  113 us
    dot_general x1, local copies, waits for them, and re-layouts, shards(): jnp.einsum('tij,tjd->tid', local_tiles, chosen, preferred_element_type=jn...  17.7 us
    dot_general x1, local copies, waits for them, and re-layouts, shards(): jnp.einsum('tji,tjd->tid', local_tiles, picked, preferred_element_type=jn...  17.7 us
    all_gather x1, blocking collectives, shards(): grad_group = lax.all_gather(grad_hidden, 'col', axis=0, tiled=True)  15.5 us
    dot_general x1, matrix products, shards(): jnp.einsum('tij,tjd->tid', local_tiles, chosen, preferred_element_type=jn...  13.1 us
    dot_general x1, matrix products, shards(): jnp.einsum('tji,tjd->tid', local_tiles, picked, preferred_element_type=jn...  12.8 us
    all_gather x1, blocking collectives, shards(): lax.all_gather(embeddings, 'row', axis=0, tiled=True)  11.6 us
    dot_general x1, matrix products, shards(): jnp.einsum('tc,tid->cid', dest_onehot, products, precision=highest)  10.8 us
  transfers between devices with their start and end apart: 3, of which 1 were waited for; matrix products, arithmetic and copies ran while one was open for 20% of the time, Pallas kernels for 0%

commit v1 on v0

--- a/solution.py
+++ b/solution.py
@@ -50,7 +50,7 @@
     weight_term = lax.dot_general(
         summed, cotangent.astype(jnp.float32), contract_rows, precision=highest
     )
-    grad_weight = lax.psum(weight_term, ("row", "col")) * scale_factor
+    grad_weight = jnp.sum(lax.all_gather(weight_term, ("row", "col")), axis=0) * scale_factor
     dest_rows = grad_group.reshape(column_count, block_rows, feature_width)
     picked = jnp.take(dest_rows, dest_ids, axis=0)
     back_products = jnp.einsum(

time: 261 us -> 199 us (0.76)
  waiting for transfers between devices: 113 us -> 48.2 us
  other arithmetic: 3.05 us -> 6.03 us
    psum x1 -> x0, waiting for transfers between devices: 113 us -> none  [shards(): grad_weight = lax.psum(weight_term, ('row', 'col')) * scale_factor]
    reduce_scatter x1, waiting for transfers between devices: 0.01 us -> 20.1 us  [shards(): lax.psum_scatter(partial_rounded.astype(jnp.float32).astype(jnp.bfloat16)...]
    reduce_scatter x1, waiting for transfers between devices: 0.01 us -> 15.2 us  [shards(): lax.psum_scatter(back_rounded.reshape(row_count * block_rows, feature_wid...]
    all_gather x0 -> x1, waiting for transfers between devices: none -> 12.9 us  [shards(): lax.all_gather(weight_term, ('row', 'col'))]
    reduce_sum x0 -> x1, other arithmetic: none -> 3.93 us  [shards(): jnp.sum(lax.all_gather(weight_term, ('row', 'col')), axis=0) * scale_factor]
  transfers between devices with their start and end apart: 3 -> 3, of which waited for: 1 -> 3; matrix products, arithmetic and copies ran while one was open for 20% -> 28% of each run, Pallas kernels for 0% -> 0%
where the time goes in v1:
time: 199 us; the launch traced here: 198 us
  matrix products  50.4 us (25%)
  local copies, waits for them, and re-layouts  50.2 us (25%)
  waiting for transfers between devices  48.2 us (24%)
  blocking collectives  26.7 us (13%)
  between operations  16.2 us (8%)
  other arithmetic  6.03 us (3%)
    reduce_scatter x1, waiting for transfers between devices, shards(): lax.psum_scatter(partial_rounded.astype(jnp.float32).astype(jnp.bfloat16)...  20.1 us
    dot_general x1, local copies, waits for them, and re-layouts, shards(): jnp.einsum('tji,tjd->tid', local_tiles, picked, preferred_element_type=jn...  17.9 us
    dot_general x1, local copies, waits for them, and re-layouts, shards(): jnp.einsum('tij,tjd->tid', local_tiles, chosen, preferred_element_type=jn...  17.7 us
    reduce_scatter x1, waiting for transfers between devices, shards(): lax.psum_scatter(back_rounded.reshape(row_count * block_rows, feature_wid...  15.2 us
    all_gather x1, blocking collectives, shards(): grad_group = lax.all_gather(grad_hidden, 'col', axis=0, tiled=True)  15.2 us
    dot_general x1, matrix products, shards(): jnp.einsum('tij,tjd->tid', local_tiles, chosen, preferred_element_type=jn...  13.1 us
    all_gather x1, waiting for transfers between devices, shards(): lax.all_gather(weight_term, ('row', 'col'))  12.9 us
    dot_general x1, matrix products, shards(): jnp.einsum('tji,tjd->tid', local_tiles, picked, preferred_element_type=jn...  12.8 us
  transfers between devices with their start and end apart: 3, of which 3 were waited for; matrix products, arithmetic and copies ran while one was open for 28% of the time, Pallas kernels for 0%

profile of v1, /device:TPU:0, one launch (start us, length us, event | category | flops | bytes accessed | tf_op | source)
XLA Modules:
  0.0 197.9 jit_solution(13044373291319878355)
XLA Ops:
  8.1 0.7 fusion.30
  8.7 0.7 compare_and_fusion.1
  9.4 11.6 %all_gather.12 = bf16[1024,256]{1,0:T(8,128)(2,1)S(1)} all-gather(bf16[128,256]{1,0:T(8,128)(2,1)} %param.7), channel_id=1, replica_groups=mesh['row'=8,'col'=4] {'row'}, dimensions={0}, use_global_device_ids=true | all-gather | bytes 589824 | tf_op jit(solution)/shard_map/all_gather | solution.py:25
  21.0 6.5 %gather_fusion = bf16[128,128,256]{2,1,0:T(8,128)(2,1)} fusion(bf16[8,128,256]{2,1,0:T(8,128)(2,1)S(1)} %bitcast.47, s32[1024]{0:T(1024)S(1)} %pad_clamp_fusion.1), kind=kCustom, calls=%fused_computation | custom fusion | bytes 16777728 | tf_op jit(solution)/shard_map/jit(_take)/gather | solution.py:28
  27.5 13.1 %fusion.6 = f32[128,256,128]{2,1,0:T(8,128)} fusion(bf16[128,128,256]{2,1,0:T(8,128)(2,1)} %gather_fusion, pred[128]{0:T(512)(128)(4,1)S(1)} %compare_and_fusion.1, bf16[1,128,128,128]{3,2,1,0:T(8,128)(2,1)} %param.10), kind=kOutput, calls=%fused_computation.8 | convolution fusion | flops 1077936128 | bytes 29360256 | tf_op jit(solution)/shard_map/tij,tjd->tid/dot_general | solution.py:29
  40.6 17.7 %copy.12 = f32[128,256,128]{1,0,2:T(8,128)} copy(f32[128,256,128]{2,1,0:T(8,128)} %fusion.6) | data formatting | bytes 33554432 | tf_op jit(solution)/shard_map/tij,tjd->tid/dot_general | solution.py:29
  59.0 10.8 %fusion.17 = bf16[4,128,256]{2,0,1:T(4,128)(2,1)S(1)} fusion(f32[128,256,128]{1,0,2:T(8,128)} %copy.12, f32[128]{0:T(128)S(1)} %compare_convert_fusion, s32[128]{0:T(128)S(1)} %bitcast.51), kind=kOutput, calls=%fused_computation.17 | convolution fusion | flops 201458688 | bytes 17040384 | tf_op jit(solution)/shard_map/tc,tid->cid/dot_general | solution.py:30
  69.8 0.7 copy.10
  70.6 0.0 all-gather.3.cloned.1.call-start
  70.7 20.1 %reduce-scatter.3.cloned.1.call-done = bf16[128,256]{1,0:T(8,128)(2,1)} async-done(((bf16[512,256]{1,0:T(8,128)(2,1)}), bf16[128,256]{1,0:T(8,128)(2,1)}) %reduce-scatter.3.cloned.1.call-update) | async-done | bytes 65552 | tf_op jit(solution)/shard_map/reduce_scatter | solution.py:34
  90.7 1.7 fusion.36
  92.5 0.0 reduce-scatter.5.cloned.1.call-start
  92.5 0.2 convolution_convert_fusion
  92.7 15.2 %all_gather.13 = bf16[512,256]{1,0:T(8,128)(2,1)S(1)} all-gather(bf16[128,256]{1,0:T(8,128)(2,1)S(1)} %convolution_convert_fusion), channel_id=1, replica_groups=mesh['row'=8,'col'=4] {'col'}, dimensions={0}, use_global_device_ids=true | all-gather | bytes 327680 | tf_op jit(solution)/shard_map/all_gather | solution.py:49
  107.9 6.5 %gather_fusion.1 = bf16[128,128,256]{2,1,0:T(8,128)(2,1)} fusion(bf16[4,128,256]{2,1,0:T(8,128)(2,1)S(1)} %bitcast.46, s32[1024]{0:T(1024)S(1)} %pad_clamp_fusion), kind=kCustom, calls=%fused_computation.1 | custom fusion | bytes 16777728 | tf_op jit(solution)/shard_map/jit(_take)/gather | solution.py:55
  114.4 12.8 %fusion.4 = f32[128,256,128]{2,1,0:T(8,128)} fusion(bf16[128,128,256]{2,1,0:T(8,128)(2,1)} %gather_fusion.1, pred[128]{0:T(512)(128)(4,1)S(1)} %compare_and_fusion, bf16[1,128,128,128]{3,2,1,0:T(8,128)(2,1)} %param.10), kind=kOutput, calls=%fused_computation.6 | convolution fusion | flops 1077936128 | bytes 29360256 | tf_op jit(solution)/shard_map/tji,tjd->tid/dot_general | solution.py:56
  127.2 17.9 %copy.13 = f32[128,256,128]{1,0,2:T(8,128)} copy(f32[128,256,128]{2,1,0:T(8,128)} %fusion.4) | data formatting | bytes 33554432 | tf_op jit(solution)/shard_map/tji,tjd->tid/dot_general | solution.py:56
  145.1 10.9 %fusion.14 = bf16[8,128,256]{2,0,1:T(8,128)(2,1)S(1)} fusion(f32[128,256,128]{1,0,2:T(8,128)} %copy.13, f32[128]{0:T(128)S(1)} %compare_convert_fusion, s32[128]{0:T(128)S(1)} %bitcast.52), kind=kOutput, calls=%fused_computation.16 | convolution fusion | flops 402917376 | bytes 17302528 | tf_op jit(solution)/shard_map/tr,tid->rid/dot_general | solution.py:59
  156.0 0.9 copy.11
  156.9 0.8 convolution_convert_fusion.1
  157.7 12.9 %all-gather.3.cloned.1.call-done = f32[8192,256]{1,0:T(8,128)} async-done(((f32[256,256]{1,0:T(8,128)}), f32[8192,256]{1,0:T(8,128)}) %all-gather.3.cloned.1.call-update) | async-done | bytes 8388624 | tf_op jit(solution)/shard_map/all_gather | solution.py:53
  170.6 3.9 %reduce_sum.9 = f32[256,256]{1,0:T(8,128)S(1)} reduce(f32[32,256,256]{2,1,0:T(8,128)} %bitcast.48, f32[]{:T(128)} %constant.28.clone.1), dimensions={0}, to_apply=%region_2.3 | reduce | flops 2031616 | bytes 8650756 | tf_op jit(solution)/shard_map/reduce_sum | solution.py:53
  174.6 0.7 broadcast_multiply_fusion
  175.3 15.2 %reduce-scatter.5.cloned.1.call-done = bf16[128,256]{1,0:T(8,128)(2,1)} async-done(((bf16[1024,256]{1,0:T(8,128)(2,1)}), bf16[128,256]{1,0:T(8,128)(2,1)}) %reduce-scatter.5.cloned.1.call-update) | async-done | bytes 65552 | tf_op jit(solution)/shard_map/reduce_scatter | solution.py:61
  (19 shorter events, 0.1 us)
Async XLA Ops:
  8.0 84.5 %copy-start = (bf16[256,256]{1,0:T(8,128)(2,1)S(1)}, bf16[256,256]{1,0:T(8,128)(2,1)}, u32[]{:S(2)}) copy-start(bf16[256,256]{1,0:T(8,128)(2,1)} %param.9) | copy-start | bytes 393220
  8.0 82.7 %reduce-scatter.3.cloned.1.call-start = ((), (), s32[]{:S(2)}) async-start(), calls=%async_computation.2 | async-start | bytes 327680 | tf_op jit(solution)/shard_map/reduce_scatter | solution.py:34
  40.6 18.4 %copy-start.3 = (s32[1,128]{1,0:T(1,128)S(1)}, s32[1,128]{1,0:T(1,128)}, u32[]{:S(2)}) copy-start(s32[1,128]{1,0:T(1,128)} %param.11) | copy-start | bytes 1540
  59.0 31.7 %copy-start.1 = (bf16[128,256]{1,0:T(8,128)(2,1)S(1)}, bf16[128,256]{1,0:T(8,128)(2,1)}, u32[]{:S(2)}) copy-start(bf16[128,256]{1,0:T(8,128)(2,1)} %param.8) | copy-start | bytes 196612
  70.6 100.0 %all-gather.3.cloned.1.call-start = ((), (), s32[]{:S(2)}) async-start(), calls=%async_computation.4 | async-start | bytes 8650752 | tf_op jit(solution)/shard_map/all_gather | solution.py:53
  92.5 98.0 %reduce-scatter.5.cloned.1.call-start = ((), (), s32[]{:S(2)}) async-start(), calls=%async_computation.3 | async-start | bytes 589824 | tf_op jit(solution)/shard_map/reduce_scatter | solution.py:61
  127.2 17.9 %copy-start.4 = (s32[1,128]{1,0:T(1,128)S(1)}, s32[1,128]{1,0:T(1,128)}, u32[]{:S(2)}) copy-start(s32[1,128]{1,0:T(1,128)} %param.12) | copy-start | bytes 1540
  145.1 11.8 %copy-start.2 = (bf16[128,256]{1,0:T(8,128)(2,1)S(1)}, bf16[128,256]{1,0:T(8,128)(2,1)}, u32[]{:S(2)}) copy-start(bf16[128,256]{1,0:T(8,128)(2,1)} %reduce-scatter.3.cloned.1.call-done) | copy-start | bytes 196612
Sparse Core Ops, SparseCore 0:
  70.7 19.9 reduce-scatter.2
  94.2 76.3 all-gather.2
Sparse Core Ops, SparseCore 1:
  157.0 33.4 reduce-scatter.4
